TPU v7x, 32 devices: a whole 2x2x4 slice. The times are simulated.
32 devices in a mesh: region: 16 (over z, y, x), blk: 2 (over core).
Axes of the slice: x: 2, y: 2, z: 4, core: 2. Of those that a mesh axis runs over, the one named last changes fastest.
Arguments:
- site_tensors: float32 [128, 2, 32, 1024], P('region', 'blk'), may hold values from -18 to 18
- projectors: bfloat16 [128, 2, 32, 1024], P('region'), may hold values from -0.1875 to 0.1875
- gate_matrix: float32 [2, 2, 2, 2], replicated, may hold values from -3 to 3
- recv_src: int32 [128, 3], P('region'), may hold values from 0 to 88, as said below
- cut_list: int32 [160], P('region'), may hold values from 0 to 23, as said below
- cut_dest: int32 [16, 10], replicated, may hold values from -1 to 63, as said below
- gate_src: int32 [128], P('region'), may hold values from 0 to 24, as said below
- gate_list: int32 [32], P('region'), may hold values from 0 to 7, as said below
- gate_dest: int32 [16, 2], replicated, may hold values from -1 to 15, as said below
Outputs:
- new_sites: float32 [128, 2, 32, 1024], P('region', 'blk')
- messages: float32 [128, 3, 1024], P('region')
Inputs may be any that keep to these rules, and one draw needn't show every extreme that they name: `recv_src`: messages between one ordered pair of regions use distinct slots below 4; some pair uses all 4. `cut_list`: entries whose cut_dest is -1 are padding. `cut_dest`: some region fills all 10 entries of its row. `gate_src`: gate partners form pairs along vertical links. `gate_list`: entries whose gate_dest is -1 are padding. `gate_dest`: some region fills all 2 entries of its row.
All inputs are finite; a program needn't handle non-finite values.
Results may differ from a plain program's by a relative error of at most 0.0039.
Values may be sent and summed in bfloat16 or wider, within the bound.
A program may use at most 128 MiB of HBM per device.

v0:
```python
import jax
import jax.numpy as jnp
from jax import lax
from jax.sharding import PartitionSpec as P

SWEEPS = 2
CAP = 4
GCAP = 1
HIGHEST = lax.Precision.HIGHEST
EPSILON = 1e-06


def weighted(tensors, incoming):
    partial_a = jnp.einsum("isabc,iag->isgbc", tensors, incoming[:, 0], precision=HIGHEST)
    return jnp.einsum("isgbc,ibe->isgec", partial_a, incoming[:, 1], precision=HIGHEST)


def outgoing(tensors, incoming):
    partial_c = jnp.einsum("isabc,icd->isabd", tensors, incoming[:, 2], precision=HIGHEST)
    both_bc = jnp.einsum("isabd,ibe->isaed", partial_c, incoming[:, 1], precision=HIGHEST)
    leg_zero = jnp.einsum("isaed,isfed->iaf", both_bc, tensors, precision=HIGHEST)
    both_ac = jnp.einsum("isabd,iag->isgbd", partial_c, incoming[:, 0], precision=HIGHEST)
    leg_one = jnp.einsum("isgbd,isghd->ibh", both_ac, tensors, precision=HIGHEST)
    both_ab = weighted(tensors, incoming)
    leg_two = jnp.einsum("isgec,isgek->ick", both_ab, tensors, precision=HIGHEST)
    return jnp.stack([leg_zero, leg_one, leg_two], axis=1)


def normalized(leg_terms):
    trace_sum = jnp.trace(leg_terms, axis1=2, axis2=3)
    return leg_terms.shape[-1] * leg_terms / trace_sum[:, :, None, None]


def select_rows(dest_table, my_region, capacity):
    region_count, columns = dest_table.shape
    wanted = my_region * capacity + jnp.arange(capacity, dtype=jnp.int32)
    matched = dest_table[:, :, None] == wanted[None, None, :]
    position = jnp.sum(
        jnp.where(matched, jnp.arange(columns, dtype=jnp.int32)[None, :, None], 0), axis=1
    )
    return (jnp.arange(region_count, dtype=jnp.int32)[:, None] * columns + position).reshape(-1)


def shards(
    site_tensors,
    projectors,
    gate_matrix,
    recv_src,
    cut_list,
    cut_dest,
    gate_src,
    gate_list,
    gate_dest,
):
    site_count = site_tensors.shape[0]
    bond_dim = site_tensors.shape[2]
    regions = lax.axis_size("region")
    my_region = lax.axis_index("region")
    my_spin = lax.axis_index("blk")
    tensors = site_tensors.reshape(site_count, 1, bond_dim, bond_dim, bond_dim)
    boundary = jnp.zeros((bond_dim, bond_dim), jnp.float32).at[0, 0].set(bond_dim)
    identity = jnp.eye(bond_dim, dtype=jnp.float32)
    msg_none = 3 * site_count + regions * CAP
    incoming = jnp.where((recv_src == msg_none)[:, :, None, None], boundary, identity)
    edge_row = boundary.reshape(1, bond_dim * bond_dim)
    for sweep_index in range(SWEEPS):
        totals = lax.psum(outgoing(tensors, incoming), "blk")
        fresh_msgs = normalized(totals).reshape(3 * site_count, bond_dim * bond_dim)
        leaving = fresh_msgs[cut_list]
        everyone = lax.all_gather(leaving, "region", axis=0, tiled=True)
        arrived = everyone[select_rows(cut_dest, my_region, CAP)]
        lookup = jnp.concatenate([fresh_msgs, arrived, edge_row], axis=0)
        incoming = lookup[recv_src].reshape(site_count, 3, bond_dim, bond_dim)
    messages = incoming.reshape(site_count, 3, bond_dim * bond_dim)
    weights = (
        weighted(tensors, incoming)
        .astype(jnp.bfloat16)
        .reshape(site_count, bond_dim * bond_dim, bond_dim)
    )
    factor = jnp.einsum(
        "ikc,isnk->icsn", weights, projectors, preferred_element_type=jnp.float32
    ).astype(jnp.bfloat16)
    factor = factor.reshape(site_count, 1, bond_dim, 2 * bond_dim)
    halves = lax.all_gather(factor, "blk", axis=1, tiled=True)
    flat_factor = halves.reshape(site_count, 4 * bond_dim * bond_dim)
    leaving_factor = flat_factor[gate_list]
    everyone_factor = lax.all_gather(leaving_factor, "region", axis=0, tiled=True)
    arrived_factor = everyone_factor[select_rows(gate_dest, my_region, GCAP)]
    empty_row = jnp.zeros((1, 4 * bond_dim * bond_dim), jnp.bfloat16)
    factor_lookup = jnp.concatenate([flat_factor, arrived_factor, empty_row], axis=0)
    partners = factor_lookup[gate_src].reshape(site_count, 2, bond_dim, 2, bond_dim)
    mixing = jnp.einsum(
        "ajby,iycjn->iabcn", gate_matrix, partners.astype(jnp.float32), precision=HIGHEST
    )
    own_old = lax.dynamic_index_in_dim(mixing, my_spin, 2, keepdims=False)
    spin_piece = jnp.einsum("iuvc,iacn->iauvn", tensors[:, 0], own_old, precision=HIGHEST)
    spin_piece = spin_piece.reshape(site_count, 2, bond_dim, bond_dim * bond_dim)
    summed = lax.psum_scatter(spin_piece, "blk", scatter_dimension=1, tiled=True)
    squares = jnp.sum(summed * summed, axis=(1, 2, 3))
    total_sq = lax.psum(squares, "blk")
    mean_sq = total_sq / (2 * bond_dim**3)
    updated = summed / jnp.sqrt(mean_sq + EPSILON)[:, None, None, None]
    unchanged = gate_src == site_count + regions * GCAP
    new_sites = jnp.where(unchanged[:, None, None, None], site_tensors, updated)
    return (new_sites, messages)


def solution(mesh):
    return jax.shard_map(
        shards,
        mesh=mesh,
        in_specs=(
            P("region", "blk", None, None),
            P("region", None, None, None),
            P(),
            P("region", None),
            P("region"),
            P(),
            P("region"),
            P("region"),
            P(),
        ),
        out_specs=(P("region", "blk", None, None), P("region", None, None)),
        check_vma=False,
    )
```

profile of v0, /device:TPU:0, one launch (start us, length us, event | category | flops | bytes accessed | tf_op | source)
XLA Modules:
  0.0 483.6 jit_solution(1316465474755128273)
XLA Ops:
  8.0 3.9 reshape.220
  11.9 6.4 %copy.94 = f32[8,32,32,32]{2,1,3,0:T(8,128)} copy(f32[8,32,32,32]{3,2,1,0:T(8,128)} %reshape.220) | data formatting | bytes 2097152 | tf_op jit(solution)/shard_map/reshape.47
  18.4 20.8 %convolution_bitcast_fusion.3 = f32[8,32,32,32]{2,3,1,0:T(8,128)S(1)} fusion(f32[8,32,32,32]{3,2,1,0:T(8,128)} %reshape.220, f32[8,3,32,32]{2,3,0,1:T(8,128)S(1)} %broadcast_select_fusion), kind=kOutput, calls=%fused_computation.35 | convolution fusion | flops 100663296 | bytes 2228224 | tf_op jit(solution)/shard_map/isabc,icd->isabd/dot_general | solution.py:19
  39.2 9.3 %fusion.14 = f32[8,32,32,32]{1,2,3,0:T(8,128)} fusion(f32[8,32,32,32]{2,3,1,0:T(8,128)S(1)} %convolution_bitcast_fusion.3, f32[8,3,32,32]{2,3,0,1:T(8,128)S(1)} %broadcast_select_fusion), kind=kOutput, calls=%fused_computation.23 | convolution fusion | flops 100663296 | bytes 5373952 | tf_op jit(solution)/shard_map/isabd,iag->isgbd/dot_general | solution.py:22
  48.5 20.6 %convolution_bitcast_fusion.2 = f32[8,32,32,32]{3,2,1,0:T(8,128)} fusion(f32[8,32,32,32]{2,3,1,0:T(8,128)S(1)} %convolution_bitcast_fusion.3, f32[8,3,32,32]{2,3,0,1:T(8,128)S(1)} %broadcast_select_fusion), kind=kOutput, calls=%fused_computation.34 | convolution fusion | flops 100663296 | bytes 5373952 | tf_op jit(solution)/shard_map/isabd,ibe->isaed/dot_general | solution.py:20
  69.1 6.8 %fusion.20 = f32[8,32,32,32]{3,1,2,0:T(8,128)} fusion(f32[8,32,32,32]{3,2,1,0:T(8,128)S(1)} %copy-done.1, f32[8,3,32,32]{2,3,0,1:T(8,128)S(1)} %broadcast_select_fusion), kind=kOutput, calls=%fused_computation.29 | convolution fusion | flops 100663296 | bytes 5373952 | tf_op jit(solution)/shard_map/isabc,iag->isgbc/dot_general | solution.py:14
  75.9 6.6 %copy.93 = f32[8,32,32,32]{2,1,3,0:T(8,128)} copy(f32[8,32,32,32]{3,2,1,0:T(8,128)} %convolution_bitcast_fusion.2) | data formatting | bytes 2097152 | tf_op jit(solution)/shard_map/reshape.51
  82.5 9.7 %convolution_bitcast_fusion.7 = f32[8,1,32,32]{3,2,0,1:T(8,128)S(1)} fusion(f32[8,32,32,32]{1,2,3,0:T(8,128)} %fusion.14, f32[8,32,32,32]{2,1,3,0:T(8,128)} %copy.94), kind=kOutput, calls=%fused_computation.43 | convolution fusion | flops 100663296 | bytes 2129920 | tf_op jit(solution)/shard_map/isgbd,isghd->ibh/dot_general | solution.py:23
  92.3 4.1 convolution_bitcast_fusion.8
  96.5 6.6 %fusion.12 = f32[8,32,32,32]{3,1,2,0:T(8,128)S(1)} fusion(f32[8,32,32,32]{3,1,2,0:T(8,128)S(1)} %copy-done.8, f32[8,3,32,32]{2,3,0,1:T(8,128)S(1)} %broadcast_select_fusion), kind=kOutput, calls=%fused_computation.21 | convolution fusion | flops 100663296 | bytes 5373952 | tf_op jit(solution)/shard_map/isgbc,ibe->isgec/dot_general | solution.py:15
  103.1 7.0 %fusion.28 = f32[8,1,32,32]{3,2,0,1:T(8,128)S(1)} fusion(f32[8,32,32,32]{3,2,1,0:T(8,128)S(1)} %copy-done.2, f32[8,32,32,32]{3,1,2,0:T(8,128)S(1)} %fusion.12), kind=kOutput, calls=%fused_computation.39 | convolution fusion | flops 100663296 | bytes 2129920 | tf_op jit(solution)/shard_map/isgec,isgek->ick/dot_general | solution.py:25
  114.8 17.5 %all-reduce.5.cloned.1.call-done = f32[8,3,32,32]{3,2,0,1:T(8,128)} async-done(((f32[8,3,32,32]{3,2,0,1:T(8,128)}), f32[8,3,32,32]{3,2,0,1:T(8,128)}) %all-reduce.5.cloned.1.call-update) | async-done | bytes 98320 | tf_op jit(solution)/shard_map/psum | solution.py:67
  135.3 49.6 %all-gather.3 = f32[16,10,1024]{2,1,0:T(8,128)} all-gather(f32[1,10,1024]{2,1,0:T(8,128)S(1)} %bitcast.197), channel_id=2, replica_groups=mesh['region'=16,'blk'=2] {'region'}, dimensions={0}, use_global_device_ids=true | all-gather | bytes 696320 | tf_op jit(solution)/shard_map/all_gather | solution.py:70
  187.8 21.2 %convolution_bitcast_fusion.1 = f32[8,32,32,32]{2,3,1,0:T(8,128)S(1)} fusion(f32[8,32,32,32]{3,2,1,0:T(8,128)} %reshape.220, f32[8,3,32,32]{3,2,1,0:T(8,128)S(1)} %reshape.224), kind=kOutput, calls=%fused_computation.33 | convolution fusion | flops 100663296 | bytes 2228224 | tf_op jit(solution)/shard_map/isabc,icd->isabd/dot_general | solution.py:19
  209.0 8.4 %fusion.10 = f32[8,32,32,32]{1,2,3,0:T(8,128)S(1)} fusion(f32[8,32,32,32]{2,3,1,0:T(8,128)S(1)} %convolution_bitcast_fusion.1, f32[8,3,32,32]{3,2,1,0:T(8,128)S(1)} %reshape.224), kind=kOutput, calls=%fused_computation.19 | convolution fusion | flops 100663296 | bytes 5373952 | tf_op jit(solution)/shard_map/isabd,iag->isgbd/dot_general | solution.py:22
  217.4 21.1 %convolution_bitcast_fusion = f32[8,32,32,32]{3,2,1,0:T(8,128)} fusion(f32[8,32,32,32]{2,3,1,0:T(8,128)S(1)} %convolution_bitcast_fusion.1, f32[8,3,32,32]{3,2,1,0:T(8,128)S(1)} %reshape.224), kind=kOutput, calls=%fused_computation.32 | convolution fusion | flops 100663296 | bytes 5373952 | tf_op jit(solution)/shard_map/isabd,ibe->isaed/dot_general | solution.py:20
  238.5 6.9 %fusion.18 = f32[8,32,32,32]{3,1,2,0:T(8,128)} fusion(f32[8,32,32,32]{3,2,1,0:T(8,128)S(1)} %copy-done.3, f32[8,3,32,32]{3,2,1,0:T(8,128)S(1)} %reshape.224), kind=kOutput, calls=%fused_computation.27 | convolution fusion | flops 100663296 | bytes 5373952 | tf_op jit(solution)/shard_map/isabc,iag->isgbc/dot_general | solution.py:14
  245.4 6.3 %convolution_bitcast_fusion.5 = f32[8,1,32,32]{3,2,0,1:T(8,128)S(1)} fusion(f32[8,32,32,32]{1,2,3,0:T(8,128)S(1)} %fusion.10, f32[8,32,32,32]{2,1,3,0:T(8,128)S(1)} %copy-done.6), kind=kOutput, calls=%fused_computation.41 | convolution fusion | flops 100663296 | bytes 2129920 | tf_op jit(solution)/shard_map/isgbd,isghd->ibh/dot_general | solution.py:23
  251.7 6.5 %copy.109 = f32[8,32,32,32]{2,1,3,0:T(8,128)} copy(f32[8,32,32,32]{3,2,1,0:T(8,128)} %convolution_bitcast_fusion) | data formatting | bytes 2097152 | tf_op jit(solution)/shard_map/reshape.70
  258.2 7.7 %convolution_bitcast_fusion.6 = f32[8,1,32,32]{3,2,0,1:T(8,128)S(1)} fusion(f32[8,32,32,32]{2,1,3,0:T(8,128)} %copy.109, f32[8,32,32,32]{2,1,3,0:T(8,128)} %copy.94), kind=kOutput, calls=%fused_computation.42 | convolution fusion | flops 100663296 | bytes 2129920 | tf_op jit(solution)/shard_map/isaed,isfed->iaf/dot_general | solution.py:21
  266.0 6.2 %fusion.8 = f32[8,32,32,32]{3,1,2,0:T(8,128)S(1)} fusion(f32[8,32,32,32]{3,1,2,0:T(8,128)S(1)} %copy-done.7, f32[8,3,32,32]{3,2,1,0:T(8,128)S(1)} %reshape.224), kind=kOutput, calls=%fused_computation.17 | convolution fusion | flops 100663296 | bytes 5373952 | tf_op jit(solution)/shard_map/isgbc,ibe->isgec/dot_general | solution.py:15
  272.2 7.2 %fusion.31 = f32[8,1,32,32]{3,2,0,1:T(8,128)S(1)} fusion(f32[8,32,32,32]{3,2,1,0:T(8,128)S(1)} %copy-done.4, f32[8,32,32,32]{3,1,2,0:T(8,128)S(1)} %fusion.8), kind=kOutput, calls=%fused_computation.40 | convolution fusion | flops 100663296 | bytes 2129920 | tf_op jit(solution)/shard_map/isgec,isgek->ick/dot_general | solution.py:25
  280.2 14.5 %all-reduce.7.cloned.1.call-done = f32[8,3,32,32]{3,2,0,1:T(8,128)} async-done(((f32[8,3,32,32]{3,2,0,1:T(8,128)}), f32[8,3,32,32]{3,2,0,1:T(8,128)}) %all-reduce.7.cloned.1.call-update) | async-done | bytes 98320 | tf_op jit(solution)/shard_map/psum | solution.py:67
  297.7 49.6 %all-gather.4 = f32[16,10,1024]{2,1,0:T(8,128)} all-gather(f32[1,10,1024]{2,1,0:T(8,128)S(1)} %bitcast.196), channel_id=3, replica_groups=mesh['region'=16,'blk'=2] {'region'}, dimensions={0}, use_global_device_ids=true | all-gather | bytes 696320 | tf_op jit(solution)/shard_map/all_gather | solution.py:70
  350.1 8.3 %fusion.16 = f32[8,32,32,32]{3,1,2,0:T(8,128)S(1)} fusion(f32[8,32,32,32]{3,2,1,0:T(8,128)} %reshape.220, f32[8,3,32,32]{3,2,1,0:T(8,128)S(1)} %reshape.228), kind=kOutput, calls=%fused_computation.25 | convolution fusion | flops 100663296 | bytes 2228224 | tf_op jit(solution)/shard_map/isabc,iag->isgbc/dot_general | solution.py:14
  358.5 5.6 %fusion.25 = bf16[8,32,32,32]{3,1,2,0:T(8,128)(2,1)S(1)} fusion(f32[8,32,32,32]{3,1,2,0:T(8,128)S(1)} %fusion.16, f32[8,3,32,32]{3,2,1,0:T(8,128)S(1)} %reshape.228), kind=kOutput, calls=%fused_computation.36 | convolution fusion | flops 100925440 | bytes 4849664 | tf_op jit(solution)/shard_map/isgbc,ibe->isgec/dot_general | solution.py:15
  368.2 37.0 %all-gather.5 = bf16[16,2,4096]{2,1,0:T(2,128)(2,1)S(1)} all-gather(bf16[1,2,4096]{2,1,0:T(2,128)(2,1)S(1)} %bitcast.198), channel_id=4, replica_groups=mesh['region'=16,'blk'=2] {'region'}, dimensions={0}, use_global_device_ids=true | all-gather | bytes 278528 | tf_op jit(solution)/shard_map/all_gather | solution.py:87
  408.2 24.5 %fusion.22 = f32[8,2,32,32,32]{3,4,2,1,0:T(8,128)} fusion(f32[8,32,32,32,1]{3,2,1,0,4:T(8,128)} %reshape.344, f32[8,2,32,32,1]{3,1,2,0,4:T(2,128)S(1)} %bitcast.195), kind=kOutput, calls=%fused_computation.31 | convolution fusion | flops 201326592 | bytes 3211264 | tf_op jit(solution)/shard_map/iuvc,iacn->iauvn/dot_general | solution.py:96
  432.7 9.0 %copy.129 = f32[8,2,32,32,32]{4,3,2,1,0:T(8,128)} copy(f32[8,2,32,32,32]{3,4,2,1,0:T(8,128)} %fusion.22) | data formatting | bytes 4194304 | tf_op jit(solution)/shard_map/iuvc,iacn->iauvn/transpose | solution.py:96
  441.6 7.7 %reshape.233 = f32[8,2,32,1024]{3,2,1,0:T(8,128)} reshape(f32[8,2,32,32,32]{4,3,2,1,0:T(8,128)} %copy.129) | data formatting | bytes 4194304 | tf_op jit(solution)/shard_map/reshape | solution.py:97
  450.0 18.5 %all-reduce.9.cloned.1.call-done = f32[8,2,32,1024]{3,2,1,0:T(8,128)} async-done(((f32[8,2,32,1024]{3,2,1,0:T(8,128)}), f32[8,2,32,1024]{3,2,1,0:T(8,128)}) %all-reduce.9.cloned.1.call-update) | async-done | bytes 2097168
  473.6 3.0 divide_select_fusion
  (121 shorter events, 30.7 us)
Async XLA Ops:
  7.2 356.9 %copy-start = (bf16[8,2,32,1024]{3,2,1,0:T(8,128)(2,1)S(1)}, bf16[8,2,32,1024]{3,2,1,0:T(8,128)(2,1)}, u32[]{:S(2)}) copy-start(bf16[8,2,32,1024]{3,2,1,0:T(8,128)(2,1)} %param.12) | copy-start | bytes 3145732
  7.2 125.1 %all-reduce.5.cloned.1.call-start = ((), (), s32[]{:S(2)}) async-start(), calls=%async_computation | async-start | bytes 786432 | tf_op jit(solution)/shard_map/psum | solution.py:67
  11.9 6.4 %copy-start.12 = (f32[32,32]{0,1:T(8,128)S(1)}, f32[32,32]{0,1:T(8,128)}, u32[]{:S(2)}) copy-start(f32[32,32]{0,1:T(8,128)} %constant.75.clone.1) | copy-start | bytes 12292
  48.5 20.6 %copy-start.1 = (f32[8,32,32,32]{3,2,1,0:T(8,128)S(1)}, f32[8,32,32,32]{3,2,1,0:T(8,128)}, u32[]{:S(2)}) copy-start(f32[8,32,32,32]{3,2,1,0:T(8,128)} %reshape.220) | copy-start | bytes 3145732
  82.5 9.8 %copy-start.5 = (f32[8,32,32,32]{2,1,3,0:T(8,128)S(1)}, f32[8,32,32,32]{2,1,3,0:T(8,128)}, u32[]{:S(2)}) copy-start(f32[8,32,32,32]{2,1,3,0:T(8,128)} %copy.94) | copy-start | bytes 3145732
  82.5 9.8 %copy-start.9 = (f32[8,32,32,32]{2,1,3,0:T(8,128)S(1)}, f32[8,32,32,32]{2,1,3,0:T(8,128)}, u32[]{:S(2)}) copy-start(f32[8,32,32,32]{2,1,3,0:T(8,128)} %copy.93) | copy-start | bytes 3145732
  92.3 4.1 copy-start.8
  96.4 6.6 %copy-start.2 = (f32[8,32,32,32]{3,2,1,0:T(8,128)S(1)}, f32[8,32,32,32]{3,2,1,0:T(8,128)}, u32[]{:S(2)}) copy-start(f32[8,32,32,32]{3,2,1,0:T(8,128)} %reshape.220) | copy-start | bytes 3145732
  103.1 7.9 %copy-start.13 = (s32[8,3]{0,1:T(4,128)S(1)}, s32[8,3]{0,1:T(4,128)}, u32[]{:S(2)}) copy-start(s32[8,3]{0,1:T(4,128)} %param.14) | copy-start | bytes 292
  103.1 8.0 %copy-start.10 = (f32[8,1,32,1024]{3,2,1,0:T(8,128)S(1)}, f32[8,1,32,1024]{3,2,1,0:T(8,128)}, u32[]{:S(2)}) copy-start(f32[8,1,32,1024]{3,2,1,0:T(8,128)} %param.11) | copy-start | bytes 3145732
  110.1 3.7 copy-start.16
  110.1 3.7 copy-start.17
  110.1 3.8 copy-start.18
  110.1 3.8 copy-start.19
  110.1 4.0 copy-start.15
  110.1 4.2 copy-start.14
  111.0 183.7 %all-reduce.7.cloned.1.call-start = ((), (), s32[]{:S(2)}) async-start(), calls=%async_computation.1 | async-start | bytes 786432 | tf_op jit(solution)/shard_map/psum | solution.py:67
  113.8 73.2 %copy-start.11 = (f32[1,1024]{1,0:T(1,128)S(1)}, f32[1,1024]{1,0:T(1,128)}, u32[]{:S(2)}) copy-start(f32[1,1024]{1,0:T(1,128)} %constant.84.clone.1) | copy-start | bytes 12292
  217.4 21.2 %copy-start.3 = (f32[8,32,32,32]{3,2,1,0:T(8,128)S(1)}, f32[8,32,32,32]{3,2,1,0:T(8,128)}, u32[]{:S(2)}) copy-start(f32[8,32,32,32]{3,2,1,0:T(8,128)} %reshape.220) | copy-start | bytes 3145732
  238.5 6.9 %copy-start.6 = (f32[8,32,32,32]{2,1,3,0:T(8,128)S(1)}, f32[8,32,32,32]{2,1,3,0:T(8,128)}, u32[]{:S(2)}) copy-start(f32[8,32,32,32]{2,1,3,0:T(8,128)} %copy.94) | copy-start | bytes 3145732
  258.2 7.7 %copy-start.7 = (f32[8,32,32,32]{3,1,2,0:T(8,128)S(1)}, f32[8,32,32,32]{3,1,2,0:T(8,128)}, u32[]{:S(2)}) copy-start(f32[8,32,32,32]{3,1,2,0:T(8,128)} %fusion.18) | copy-start | bytes 3145732
  266.0 6.2 %copy-start.4 = (f32[8,32,32,32]{3,2,1,0:T(8,128)S(1)}, f32[8,32,32,32]{3,2,1,0:T(8,128)}, u32[]{:S(2)}) copy-start(f32[8,32,32,32]{3,2,1,0:T(8,128)} %reshape.220) | copy-start | bytes 3145732
  280.2 188.3 %all-reduce.9.cloned.1.call-start = ((), (), s32[]{:S(2)}) async-start(), calls=%async_computation.2 | async-start | bytes 4194304
  441.6 7.7 %copy-start.20 = (u32[32]{0:T(128)S(1)}, u32[32]{0:T(128)}, u32[]{:S(2)}) copy-start(u32[32]{0:T(128)} %constant.101) | copy-start | bytes 388
Sparse Core Ops, SparseCore 0:
  111.1 21.1 all-reduce.4
  280.3 14.3 all-reduce.6
  449.5 19.0 all-reduce.8
where the time goes:
time: 492 us; the launch traced here: 484 us
  matrix products  210 us (43%)
  blocking collectives  141 us (29%)
  local copies, waits for them, and re-layouts  54.7 us (11%)
  waiting for transfers between devices  50.5 us (10%)
  between operations  14.8 us (3%)
  other arithmetic  12.3 us (2%)
    all_gather x2, blocking collectives, shards(): everyone = lax.all_gather(leaving, 'region', axis=0, tiled=True)  99.2 us
    dot_general x2, matrix products, outgoing(): jnp.einsum('isabc,icd->isabd', tensors, incoming[:, 2], precision=HIGHEST)  42 us
    dot_general x2, matrix products, outgoing(): jnp.einsum('isabd,ibe->isaed', partial_c, incoming[:, 1], precision=HIGHEST)  41.8 us
    all_gather x1, blocking collectives, shards(): lax.all_gather(leaving_factor, 'region', axis=0, tiled=True)  37 us
    psum x2, waiting for transfers between devices, shards(): totals = lax.psum(outgoing(tensors, incoming), 'blk')  32 us
    another operation x6, local copies, waits for them, and re-layouts  26.4 us
    dot_general x1, matrix products, shards(): jnp.einsum('iuvc,iacn->iauvn', tensors[:, 0], own_old, precision=HIGHEST)  24.5 us
    dot_general x3, matrix products, weighted(): jnp.einsum('isabc,iag->isgbc', tensors, incoming[:, 0], precision=HIGHEST)  22.1 us
  transfers between devices with their start and end apart: 3, of which 3 were waited for; matrix products, arithmetic and copies ran while one was open for 1% of the time, Pallas kernels for 0%

commit v1 on v0

--- a/solution.py
+++ b/solution.py
@@ -64,7 +64,8 @@
     incoming = jnp.where((recv_src == msg_none)[:, :, None, None], boundary, identity)
     edge_row = boundary.reshape(1, bond_dim * bond_dim)
     for sweep_index in range(SWEEPS):
-        totals = lax.psum(outgoing(tensors, incoming), "blk")
+        store_map = lambda vals, axis_name: lax.all_gather(vals, axis_name=axis_name).sum(axis=0)
+        totals = store_map(outgoing(tensors, incoming), "blk")
         fresh_msgs = normalized(totals).reshape(3 * site_count, bond_dim * bond_dim)
         leaving = fresh_msgs[cut_list]
         everyone = lax.all_gather(leaving, "region", axis=0, tiled=True)

time: 492 us -> 463 us (0.941)
  waiting for transfers between devices: 50.5 us -> 16.5 us
  matrix products: 210 us -> 215 us
    psum x2 -> x0, waiting for transfers between devices: 32 us -> none  [shards(): totals = lax.psum(outgoing(tensors, incoming), 'blk')]
    all_gather x2, blocking collectives: 99.2 us -> 92.8 us  [shards(): everyone = lax.all_gather(leaving, 'region', axis=0, tiled=True)]
    unnamed x4 -> x2, waiting for transfers between devices: 18.6 us -> 16.5 us
  transfers between devices with their start and end apart: 3 -> 1, of which waited for: 3 -> 1; matrix products, arithmetic and copies ran while one was open for 1% -> 0% of each run, Pallas kernels for 0% -> 0%
where the time goes in v1:
time: 463 us; the launch traced here: 454 us
  matrix products  215 us (46%)
  blocking collectives  141 us (30%)
  local copies, waits for them, and re-layouts  55.2 us (12%)
  waiting for transfers between devices  16.5 us (4%)
  between operations  15 us (3%)
  other arithmetic  11.3 us (2%)
    all_gather x2, blocking collectives, shards(): everyone = lax.all_gather(leaving, 'region', axis=0, tiled=True)  92.8 us
    dot_general x2, matrix products, outgoing(): jnp.einsum('isabc,icd->isabd', tensors, incoming[:, 2], precision=HIGHEST)  42 us
    dot_general x2, matrix products, outgoing(): jnp.einsum('isabd,ibe->isaed', partial_c, incoming[:, 1], precision=HIGHEST)  41.8 us
    all_gather x1, blocking collectives, shards(): lax.all_gather(leaving_factor, 'region', axis=0, tiled=True)  39.2 us
    another operation x6, local copies, waits for them, and re-layouts  26.6 us
    dot_general x1, matrix products, shards(): jnp.einsum('iuvc,iacn->iauvn', tensors[:, 0], own_old, precision=HIGHEST)  24.5 us
    dot_general x3, matrix products, weighted(): jnp.einsum('isabc,iag->isgbc', tensors, incoming[:, 0], precision=HIGHEST)  22.1 us
    dot_general x2, matrix products, outgoing(): jnp.einsum('isgbd,isghd->ibh', both_ac, tensors, precision=HIGHEST)  19.5 us
  transfers between devices with their start and end apart: 1, of which 1 were waited for; matrix products, arithmetic and copies ran while one was open for 0% of the time, Pallas kernels for 0%

profile of v1, /device:TPU:0, one launch (start us, length us, event | category | flops | bytes accessed | tf_op | source)
XLA Modules:
  0.0 454.2 jit_solution(2003061511765591170)
XLA Ops:
  8.7 3.9 reshape.226
  12.6 6.4 %copy.131 = f32[8,32,32,32]{2,1,3,0:T(8,128)} copy(f32[8,32,32,32]{3,2,1,0:T(8,128)} %reshape.226) | data formatting | bytes 2097152 | tf_op jit(solution)/shard_map/reshape.47
  19.1 20.8 %convolution_bitcast_fusion.3 = f32[8,32,32,32]{2,3,1,0:T(8,128)S(1)} fusion(f32[8,32,32,32]{3,2,1,0:T(8,128)} %reshape.226, f32[8,3,32,32]{2,3,0,1:T(8,128)S(1)} %broadcast_select_fusion), kind=kOutput, calls=%fused_computation.35 | convolution fusion | flops 100663296 | bytes 2228224 | tf_op jit(solution)/shard_map/isabc,icd->isabd/dot_general | solution.py:19
  39.9 9.3 %fusion.14 = f32[8,32,32,32]{1,2,3,0:T(8,128)} fusion(f32[8,32,32,32]{2,3,1,0:T(8,128)S(1)} %convolution_bitcast_fusion.3, f32[8,3,32,32]{2,3,0,1:T(8,128)S(1)} %broadcast_select_fusion), kind=kOutput, calls=%fused_computation.23 | convolution fusion | flops 100663296 | bytes 5373952 | tf_op jit(solution)/shard_map/isabd,iag->isgbd/dot_general | solution.py:22
  49.2 20.7 %convolution_bitcast_fusion.2 = f32[8,32,32,32]{3,2,1,0:T(8,128)} fusion(f32[8,32,32,32]{2,3,1,0:T(8,128)S(1)} %convolution_bitcast_fusion.3, f32[8,3,32,32]{2,3,0,1:T(8,128)S(1)} %broadcast_select_fusion), kind=kOutput, calls=%fused_computation.34 | convolution fusion | flops 100663296 | bytes 5373952 | tf_op jit(solution)/shard_map/isabd,ibe->isaed/dot_general | solution.py:20
  69.9 6.8 %fusion.20 = f32[8,32,32,32]{3,1,2,0:T(8,128)} fusion(f32[8,32,32,32]{3,2,1,0:T(8,128)S(1)} %copy-done.1, f32[8,3,32,32]{2,3,0,1:T(8,128)S(1)} %broadcast_select_fusion), kind=kOutput, calls=%fused_computation.29 | convolution fusion | flops 100663296 | bytes 5373952 | tf_op jit(solution)/shard_map/isabc,iag->isgbc/dot_general | solution.py:14
  77.4 6.8 %copy.130 = f32[8,32,32,32]{2,1,3,0:T(8,128)} copy(f32[8,32,32,32]{3,2,1,0:T(8,128)} %convolution_bitcast_fusion.2) | data formatting | bytes 2097152 | tf_op jit(solution)/shard_map/reshape.51
  84.2 9.8 %convolution_bitcast_fusion.7 = f32[8,1,32,32]{3,2,0,1:T(8,128)S(1)} fusion(f32[8,32,32,32]{1,2,3,0:T(8,128)} %fusion.14, f32[8,32,32,32]{2,1,3,0:T(8,128)} %copy.131), kind=kOutput, calls=%fused_computation.43 | convolution fusion | flops 100663296 | bytes 2129920 | tf_op jit(solution)/shard_map/isgbd,isghd->ibh/dot_general | solution.py:23
  94.1 4.1 convolution_bitcast_fusion.8
  98.2 6.3 %fusion.12 = f32[8,32,32,32]{3,1,2,0:T(8,128)S(1)} fusion(f32[8,32,32,32]{3,1,2,0:T(8,128)S(1)} %copy-done.6, f32[8,3,32,32]{2,3,0,1:T(8,128)S(1)} %broadcast_select_fusion), kind=kOutput, calls=%fused_computation.21 | convolution fusion | flops 100663296 | bytes 5373952 | tf_op jit(solution)/shard_map/isgbc,ibe->isgec/dot_general | solution.py:15
  104.5 7.0 %fusion.28 = f32[8,1,32,32]{3,2,0,1:T(8,128)S(1)} fusion(f32[8,32,32,32]{3,2,1,0:T(8,128)S(1)} %copy-done.2, f32[8,32,32,32]{3,1,2,0:T(8,128)S(1)} %fusion.12), kind=kOutput, calls=%fused_computation.39 | convolution fusion | flops 100663296 | bytes 2129920 | tf_op jit(solution)/shard_map/isgec,isgek->ick/dot_general | solution.py:25
  111.6 2.5 all-gather
  115.4 49.0 %all-gather.5 = f32[16,10,1024]{2,1,0:T(8,128)S(1)} all-gather(f32[1,10,1024]{2,1,0:T(8,128)S(1)} %bitcast.201), channel_id=3, replica_groups=mesh['region'=16,'blk'=2] {'region'}, dimensions={0}, use_global_device_ids=true | all-gather | bytes 696320 | tf_op jit(solution)/shard_map/all_gather | solution.py:71
  165.9 21.3 %convolution_bitcast_fusion.1 = f32[8,32,32,32]{2,3,1,0:T(8,128)S(1)} fusion(f32[8,32,32,32]{3,2,1,0:T(8,128)} %reshape.226, f32[8,3,32,32]{3,2,1,0:T(8,128)S(1)} %reshape.229), kind=kOutput, calls=%fused_computation.33 | convolution fusion | flops 100663296 | bytes 2228224 | tf_op jit(solution)/shard_map/isabc,icd->isabd/dot_general | solution.py:19
  187.2 9.3 %fusion.10 = f32[8,32,32,32]{1,2,3,0:T(8,128)} fusion(f32[8,32,32,32]{2,3,1,0:T(8,128)S(1)} %convolution_bitcast_fusion.1, f32[8,3,32,32]{3,2,1,0:T(8,128)S(1)} %reshape.229), kind=kOutput, calls=%fused_computation.19 | convolution fusion | flops 100663296 | bytes 5373952 | tf_op jit(solution)/shard_map/isabd,iag->isgbd/dot_general | solution.py:22
  196.5 21.1 %convolution_bitcast_fusion = f32[8,32,32,32]{3,2,1,0:T(8,128)} fusion(f32[8,32,32,32]{2,3,1,0:T(8,128)S(1)} %convolution_bitcast_fusion.1, f32[8,3,32,32]{3,2,1,0:T(8,128)S(1)} %reshape.229), kind=kOutput, calls=%fused_computation.32 | convolution fusion | flops 100663296 | bytes 5373952 | tf_op jit(solution)/shard_map/isabd,ibe->isaed/dot_general | solution.py:20
  217.6 6.9 %fusion.18 = f32[8,32,32,32]{3,1,2,0:T(8,128)} fusion(f32[8,32,32,32]{3,2,1,0:T(8,128)S(1)} %copy-done.3, f32[8,3,32,32]{3,2,1,0:T(8,128)S(1)} %reshape.229), kind=kOutput, calls=%fused_computation.27 | convolution fusion | flops 100663296 | bytes 5373952 | tf_op jit(solution)/shard_map/isabc,iag->isgbc/dot_general | solution.py:14
  224.6 2.7 reshape.350
  229.9 9.7 %convolution_bitcast_fusion.5 = f32[8,1,32,32]{3,2,0,1:T(8,128)S(1)} fusion(f32[8,32,32,32]{1,2,3,0:T(8,128)} %fusion.10, f32[8,32,32,32]{2,1,3,0:T(8,128)} %copy.131), kind=kOutput, calls=%fused_computation.41 | convolution fusion | flops 100663296 | bytes 2129920 | tf_op jit(solution)/shard_map/isgbd,isghd->ibh/dot_general | solution.py:23
  239.6 6.5 %copy.147 = f32[8,32,32,32]{2,1,3,0:T(8,128)} copy(f32[8,32,32,32]{3,2,1,0:T(8,128)} %convolution_bitcast_fusion) | data formatting | bytes 2097152 | tf_op jit(solution)/shard_map/reshape.70
  246.1 7.7 %convolution_bitcast_fusion.6 = f32[8,1,32,32]{3,2,0,1:T(8,128)S(1)} fusion(f32[8,32,32,32]{2,1,3,0:T(8,128)} %copy.147, f32[8,32,32,32]{2,1,3,0:T(8,128)} %copy.131), kind=kOutput, calls=%fused_computation.42 | convolution fusion | flops 100663296 | bytes 2129920 | tf_op jit(solution)/shard_map/isaed,isfed->iaf/dot_general | solution.py:21
  253.8 6.2 %fusion.8 = f32[8,32,32,32]{3,1,2,0:T(8,128)S(1)} fusion(f32[8,32,32,32]{3,1,2,0:T(8,128)S(1)} %copy-done.7, f32[8,3,32,32]{3,2,1,0:T(8,128)S(1)} %reshape.229), kind=kOutput, calls=%fused_computation.17 | convolution fusion | flops 100663296 | bytes 5373952 | tf_op jit(solution)/shard_map/isgbc,ibe->isgec/dot_general | solution.py:15
  260.0 7.2 %fusion.31 = f32[8,1,32,32]{3,2,0,1:T(8,128)S(1)} fusion(f32[8,32,32,32]{3,2,1,0:T(8,128)S(1)} %copy-done.4, f32[8,32,32,32]{3,1,2,0:T(8,128)S(1)} %fusion.8), kind=kOutput, calls=%fused_computation.40 | convolution fusion | flops 100663296 | bytes 2129920 | tf_op jit(solution)/shard_map/isgec,isgek->ick/dot_general | solution.py:25
  272.8 43.8 %all-gather.6 = f32[16,10,1024]{2,1,0:T(8,128)} all-gather(f32[1,10,1024]{2,1,0:T(8,128)S(1)} %bitcast.200), channel_id=5, replica_groups=mesh['region'=16,'blk'=2] {'region'}, dimensions={0}, use_global_device_ids=true | all-gather | bytes 696320 | tf_op jit(solution)/shard_map/all_gather | solution.py:71
  319.4 8.3 %fusion.16 = f32[8,32,32,32]{3,1,2,0:T(8,128)S(1)} fusion(f32[8,32,32,32]{3,2,1,0:T(8,128)} %reshape.226, f32[8,3,32,32]{3,2,1,0:T(8,128)S(1)} %reshape.232), kind=kOutput, calls=%fused_computation.25 | convolution fusion | flops 100663296 | bytes 2228224 | tf_op jit(solution)/shard_map/isabc,iag->isgbc/dot_general | solution.py:14
  327.7 5.6 %fusion.25 = bf16[8,32,32,32]{3,1,2,0:T(8,128)(2,1)S(1)} fusion(f32[8,32,32,32]{3,1,2,0:T(8,128)S(1)} %fusion.16, f32[8,3,32,32]{3,2,1,0:T(8,128)S(1)} %reshape.232), kind=kOutput, calls=%fused_computation.36 | convolution fusion | flops 100925440 | bytes 4849664 | tf_op jit(solution)/shard_map/isgbc,ibe->isgec/dot_general | solution.py:15
  337.6 39.2 %all-gather.7 = bf16[16,2,4096]{2,1,0:T(2,128)(2,1)S(1)} all-gather(bf16[1,2,4096]{2,1,0:T(2,128)(2,1)S(1)} %bitcast.202), channel_id=6, replica_groups=mesh['region'=16,'blk'=2] {'region'}, dimensions={0}, use_global_device_ids=true | all-gather | bytes 278528 | tf_op jit(solution)/shard_map/all_gather | solution.py:88
  380.1 24.5 %fusion.22 = f32[8,2,32,32,32]{3,4,2,1,0:T(8,128)} fusion(f32[8,32,32,32,1]{3,2,1,0,4:T(8,128)} %reshape.350, f32[8,2,32,32,1]{3,1,2,0,4:T(2,128)S(1)} %bitcast.199), kind=kOutput, calls=%fused_computation.31 | convolution fusion | flops 201326592 | bytes 3211264 | tf_op jit(solution)/shard_map/iuvc,iacn->iauvn/dot_general | solution.py:97
  404.7 9.0 %copy.168 = f32[8,2,32,32,32]{4,3,2,1,0:T(8,128)} copy(f32[8,2,32,32,32]{3,4,2,1,0:T(8,128)} %fusion.22) | data formatting | bytes 4194304 | tf_op jit(solution)/shard_map/iuvc,iacn->iauvn/transpose | solution.py:97
  413.7 7.7 %reshape.237 = f32[8,2,32,1024]{3,2,1,0:T(8,128)} reshape(f32[8,2,32,32,32]{4,3,2,1,0:T(8,128)} %copy.168) | data formatting | bytes 4194304 | tf_op jit(solution)/shard_map/reshape | solution.py:98
  422.2 16.5 %all-reduce.3.cloned.1.call-done = f32[8,2,32,1024]{3,2,1,0:T(8,128)} async-done(((f32[8,2,32,1024]{3,2,1,0:T(8,128)}), f32[8,2,32,1024]{3,2,1,0:T(8,128)}) %all-reduce.3.cloned.1.call-update) | async-done | bytes 2097168
  443.9 3.1 divide_select_fusion
  (125 shorter events, 29.4 us)
Async XLA Ops:
  7.2 326.2 %copy-start = (bf16[8,2,32,1024]{3,2,1,0:T(8,128)(2,1)S(1)}, bf16[8,2,32,1024]{3,2,1,0:T(8,128)(2,1)}, u32[]{:S(2)}) copy-start(bf16[8,2,32,1024]{3,2,1,0:T(8,128)(2,1)} %param.12) | copy-start | bytes 3145732
  7.2 431.5 %all-reduce.3.cloned.1.call-start = ((), (), s32[]{:S(2)}) async-start(), calls=%async_computation | async-start | bytes 4194304
  12.6 6.4 %copy-start.11 = (f32[32,32]{0,1:T(8,128)S(1)}, f32[32,32]{0,1:T(8,128)}, u32[]{:S(2)}) copy-start(f32[32,32]{0,1:T(8,128)} %constant.75.clone.1) | copy-start | bytes 12292
  49.2 20.7 %copy-start.1 = (f32[8,32,32,32]{3,2,1,0:T(8,128)S(1)}, f32[8,32,32,32]{3,2,1,0:T(8,128)}, u32[]{:S(2)}) copy-start(f32[8,32,32,32]{3,2,1,0:T(8,128)} %reshape.226) | copy-start | bytes 3145732
  69.9 6.8 %copy-start.17 = (s32[10]{0:T(128)S(1)}, s32[10]{0:T(128)}, u32[]{:S(2)}) copy-start(s32[10]{0:T(128)} %param.15) | copy-start | bytes 124
  69.9 7.1 %copy-start.12 = (s32[16,10]{1,0:T(8,128)S(1)}, s32[16,10]{1,0:T(8,128)}, u32[]{:S(2)}) copy-start(s32[16,10]{1,0:T(8,128)} %param.16) | copy-start | bytes 1924
  76.9 37.9 %copy-start.13 = (s32[1024]{0:T(1024)}, s32[1024]{0:T(1024)S(1)}, u32[]{:S(2)}) copy-start(s32[1024]{0:T(1024)S(1)} %pad_clamp_fusion.5) | copy-start | bytes 12292
  84.2 9.9 %copy-start.5 = (f32[8,32,32,32]{2,1,3,0:T(8,128)S(1)}, f32[8,32,32,32]{2,1,3,0:T(8,128)}, u32[]{:S(2)}) copy-start(f32[8,32,32,32]{2,1,3,0:T(8,128)} %copy.131) | copy-start | bytes 3145732
  84.2 9.9 %copy-start.8 = (f32[8,32,32,32]{2,1,3,0:T(8,128)S(1)}, f32[8,32,32,32]{2,1,3,0:T(8,128)}, u32[]{:S(2)}) copy-start(f32[8,32,32,32]{2,1,3,0:T(8,128)} %copy.130) | copy-start | bytes 3145732
  94.1 4.1 copy-start.6
  98.2 6.3 %copy-start.2 = (f32[8,32,32,32]{3,2,1,0:T(8,128)S(1)}, f32[8,32,32,32]{3,2,1,0:T(8,128)}, u32[]{:S(2)}) copy-start(f32[8,32,32,32]{3,2,1,0:T(8,128)} %reshape.226) | copy-start | bytes 3145732
  114.1 51.0 %copy-start.10 = (f32[1,1024]{1,0:T(1,128)S(1)}, f32[1,1024]{1,0:T(1,128)}, u32[]{:S(2)}) copy-start(f32[1,1024]{1,0:T(1,128)} %constant.84.clone.1) | copy-start | bytes 12292
  196.5 21.1 %copy-start.3 = (f32[8,32,32,32]{3,2,1,0:T(8,128)S(1)}, f32[8,32,32,32]{3,2,1,0:T(8,128)}, u32[]{:S(2)}) copy-start(f32[8,32,32,32]{3,2,1,0:T(8,128)} %reshape.226) | copy-start | bytes 3145732
  217.6 6.9 %copy-start.9 = (f32[8,1,32,1024]{3,2,1,0:T(8,128)S(1)}, f32[8,1,32,1024]{3,2,1,0:T(8,128)}, u32[]{:S(2)}) copy-start(f32[8,1,32,1024]{3,2,1,0:T(8,128)} %param.11) | copy-start | bytes 3145732
  224.6 2.7 copy-start.16
  224.6 2.8 copy-start.18
  224.6 2.8 copy-start.19
  224.6 4.6 %copy-start.14 = (f32[2,2,2,2]{3,2,1,0:T(2,128)S(1)}, f32[2,2,2,2]{3,2,1,0:T(2,128)}, u32[]{:S(2)}) copy-start(f32[2,2,2,2]{3,2,1,0:T(2,128)} %param.13) | copy-start | bytes 196
  246.1 7.7 %copy-start.7 = (f32[8,32,32,32]{3,1,2,0:T(8,128)S(1)}, f32[8,32,32,32]{3,1,2,0:T(8,128)}, u32[]{:S(2)}) copy-start(f32[8,32,32,32]{3,1,2,0:T(8,128)} %fusion.18) | copy-start | bytes 3145732
  253.8 6.2 %copy-start.4 = (f32[8,32,32,32]{3,2,1,0:T(8,128)S(1)}, f32[8,32,32,32]{3,2,1,0:T(8,128)}, u32[]{:S(2)}) copy-start(f32[8,32,32,32]{3,2,1,0:T(8,128)} %reshape.226) | copy-start | bytes 3145732
  333.4 45.4 %copy-start.15 = (f32[2,2,2,2,1,1]{1,2,3,0,5,4:T(2,128)S(1)}, f32[2,2,2,2,1,1]{1,2,3,0,5,4:T(2,128)}, u32[]{:S(2)}) copy-start(f32[2,2,2,2,1,1]{1,2,3,0,5,4:T(2,128)} %copy.192) | copy-start | bytes 196
  413.7 7.8 %copy-start.21 = (u32[32]{0:T(128)S(1)}, u32[32]{0:T(128)}, u32[]{:S(2)}) copy-start(u32[32]{0:T(128)} %constant.101) | copy-start | bytes 388
  413.7 8.4 %copy-start.20 = (s32[8]{0:T(128)S(1)}, s32[8]{0:T(128)}, u32[]{:S(2)}) copy-start(s32[8]{0:T(128)} %param.17) | copy-start | bytes 100
Sparse Core Ops, SparseCore 0:
  421.6 17.0 all-reduce.2
